TPU v7x, 512 devices: a whole 4x4x16 slice. The times are simulated.
512 devices in a mesh: blk: 128 (over x, z, core), gz: 4 (over y).
Axes of the slice: x: 4, y: 4, z: 16, core: 2. Of those that a mesh axis runs over, the one named last changes fastest.
Arguments:
- fixed: bfloat16 [128, 32, 32, 128], P('blk', 'gz'), may hold values from -6 to 6
- moving: bfloat16 [128, 32, 32, 128], P('blk', 'gz'), may hold values from -6 to 6
- block_place: int32 [128], P('blk'), may hold values from 0 to 127, each once
- tissue: int32 [128], P('blk'), may hold values 0 or 1
Outputs:
- velocity: float32 [3, 2, 32, 64], replicated
- cc_map: float32 [128, 32, 32, 128], P('blk', 'gz')
Inputs may be any that keep to these rules, and one draw needn't show every extreme that they name: `block_place`: each block position from 0 to 127 is named by exactly one block.
All inputs are finite; a program needn't handle non-finite values. No bound on the sum of `tissue` on one device may be relied on, other than what follows from the above.
Results may differ from a plain program's by a relative error of at most 0.0004.
Values may be sent and summed in bfloat16 or wider, within the bound.
A program may use at most 64 MiB of HBM per device.

v0:
```python
import math
import jax
import jax.numpy as jnp
from jax import lax
from jax.sharding import PartitionSpec as P

SCALE = 16
GY = 8
ITERS = 2
EXACT = lax.Precision.HIGHEST
EPSILON = 1e-05
STEP_LENGTH = 0.5
BOX_TAPS = [1.0 / 9.0] * 9
GAUSS_RAW = [math.exp(-((offset - 3) ** 2) / 4.5) for offset in range(7)]
GAUSS_TAPS = [value / sum(GAUSS_RAW) for value in GAUSS_RAW]


def with_halo(block, sides, width):
    for axis, dim in sides:
        count = lax.axis_size(axis)
        forward = [(i, i + 1) for i in range(count - 1)]
        backward = [(target, source) for source, target in forward]
        low = lax.ppermute(
            lax.slice_in_dim(block, block.shape[dim] - width, None, axis=dim), axis, forward
        )
        high = lax.ppermute(lax.slice_in_dim(block, 0, width, axis=dim), axis, backward)
        block = jnp.concatenate([low, block, high], axis=dim)
    return block


def tap_matrix(count, taps):
    radius = len(taps) // 2
    rows = jnp.arange(count)[:, None]
    cols = jnp.arange(count)[None, :]
    matrix = jnp.zeros((count, count), jnp.float32)
    for offset, weight in enumerate(taps):
        matrix = matrix + weight * (rows - cols == offset - radius).astype(jnp.float32)
    return matrix


def along_rows(field, matrix):
    return jnp.einsum("...xy,xu->...uy", field, matrix, precision=EXACT)


def along_cols(field, matrix):
    return jnp.einsum("...y,yv->...v", field, matrix, precision=EXACT)


def planes_filter(field, taps, count):
    total = jnp.zeros(field.shape[:-3] + (count,) + field.shape[-2:], jnp.float32)
    for offset, weight in enumerate(taps):
        total = total + weight * field[..., offset : offset + count, :, :]
    return total


def slope(field, axis):
    widths = [(0, 0)] * field.ndim
    widths[axis] = (1, 1)
    padded = jnp.pad(field, widths)
    length = field.shape[axis]
    upper = lax.slice_in_dim(padded, 2, length + 2, axis=axis)
    lower = lax.slice_in_dim(padded, 0, length, axis=axis)
    return 0.5 * (upper - lower)


def hat_rows(coords, count):
    where = jnp.clip((coords + 0.5) / SCALE - 0.5, 0.0, count - 1.0)
    marks = jnp.arange(count).astype(jnp.float32)
    return jnp.maximum(0.0, 1.0 - jnp.abs(where[..., None] - marks))


def statistics(means, fixed_c, warped_c):
    sii = means[2] - means[0] * means[0]
    sww = means[3] - means[1] * means[1]
    siw = means[4] - means[0] * means[1]
    denom = sii * sww + EPSILON
    similar = siw * siw / denom
    weight = (
        2.0 * siw / denom * (fixed_c - means[0] - siw / (sww + EPSILON) * (warped_c - means[1]))
    )
    return (similar, weight)


def smooth_axis(field, axis):
    widths = [(0, 0)] * field.ndim
    widths[axis] = (1, 1)
    padded = jnp.pad(field, widths)
    length = field.shape[axis]
    upper = lax.slice_in_dim(padded, 2, length + 2, axis=axis)
    lower = lax.slice_in_dim(padded, 0, length, axis=axis)
    return 0.25 * lower + 0.5 * field + 0.25 * upper


def regularize(velocity, total, coarse_rows, coarse_cols):
    block_rows = velocity.shape[2] // coarse_rows
    coarse_depth = velocity.shape[1]
    grid = total.reshape(block_rows, GY, 3, coarse_depth, coarse_rows, coarse_cols)
    grid = grid.transpose(2, 3, 0, 4, 1, 5).reshape(velocity.shape)
    regular = smooth_axis(smooth_axis(smooth_axis(grid, 1), 2), 3)
    return velocity + STEP_LENGTH * regular / jnp.sqrt(jnp.mean(regular * regular) + EPSILON)


def per_device(fixed, moving, block_place, tissue):
    slots, planes, row_side, col_side = fixed.shape
    depth_parts = lax.axis_size("gz")
    depth_index = lax.axis_index("gz")
    blocks = slots * lax.axis_size("blk")
    total_planes = planes * depth_parts
    coarse_depth = total_planes // SCALE
    coarse_rows = row_side // SCALE
    coarse_cols = col_side // SCALE
    grid_rows = blocks // GY * coarse_rows
    grid_cols = GY * coarse_cols
    stacked = jnp.stack([fixed, moving], 0)
    reach = 0
    haloed = with_halo(stacked, (("gz", 2),), 5)
    images = haloed.astype(jnp.float32)
    count_w = planes + 2 * (reach + 4)
    count_m = planes + 2 * reach
    fixed_w = images[0, :, 1 : 1 + count_w]
    moving_w = images[1, :, 1 : 1 + count_w]
    depth_slope = 0.5 * (images[1, :, 2 : 2 + count_w] - images[1, :, 0:count_w])
    row_slope = slope(moving_w, 2)
    col_slope = slope(moving_w, 3)
    depth_w = depth_index * planes - (reach + 4) + jnp.arange(count_w)
    inside_w = ((depth_w >= 0) & (depth_w < total_planes)).astype(jnp.float32)
    depth_hat = hat_rows(depth_w.astype(jnp.float32), coarse_depth)
    depth_m = depth_index * planes - reach + jnp.arange(count_m)
    inside_m = ((depth_m >= 0) & (depth_m < total_planes)).astype(jnp.float32)
    row_cells = jnp.arange(row_side)
    col_cells = jnp.arange(col_side)
    block_row = block_place // GY
    block_col = block_place % GY
    row_hat = hat_rows(
        (block_row[:, None] * row_side + row_cells[None, :]).astype(jnp.float32), grid_rows
    )
    col_hat = hat_rows(
        (block_col[:, None] * col_side + col_cells[None, :]).astype(jnp.float32), grid_cols
    )
    own_depth = depth_index * planes + jnp.arange(planes)
    restrict = (own_depth[None, :] // SCALE == jnp.arange(coarse_depth)[:, None]).astype(
        jnp.float32
    )
    box_rows = tap_matrix(row_side, BOX_TAPS)
    box_cols = tap_matrix(col_side, BOX_TAPS)
    gauss_rows = tap_matrix(row_side, GAUSS_TAPS)
    gauss_cols = tap_matrix(col_side, GAUSS_TAPS)
    tissue_scale = tissue.astype(jnp.float32)[:, None, None, None]
    positions = jnp.arange(blocks)
    velocity = jnp.zeros((3, coarse_depth, grid_rows, grid_cols), jnp.float32)
    correlation = jnp.zeros((slots, planes, row_side, col_side), jnp.float32)
    for rounds in range(ITERS):
        partial_value = jnp.einsum("ckab,sxa->sckxb", velocity, row_hat, precision=EXACT)
        partial_value = jnp.einsum("sckxb,syb->sckxy", partial_value, col_hat, precision=EXACT)
        shift = jnp.einsum("zk,sckxy->cszxy", depth_hat, partial_value, precision=EXACT)
        warped = moving_w + shift[0] * depth_slope + shift[1] * row_slope + shift[2] * col_slope
        warped = warped * inside_w[None, :, None, None]
        fields = jnp.stack(
            [fixed_w, warped, fixed_w * fixed_w, warped * warped, fixed_w * warped], 0
        )
        means = planes_filter(fields, BOX_TAPS, count_m)
        means = along_cols(along_rows(means, box_rows), box_cols)
        fixed_m = fixed_w[:, 4 : 4 + count_m]
        warped_m = warped[:, 4 : 4 + count_m]
        similar, weight = statistics(means, fixed_m, warped_m)
        scale = weight * tissue_scale * inside_m[None, :, None, None]
        depth_grad = 0.5 * (warped[:, 5 : 5 + count_m] - warped[:, 3 : 3 + count_m])
        force = jnp.stack(
            [scale * depth_grad, scale * slope(warped_m, 2), scale * slope(warped_m, 3)], 0
        )
        force = with_halo(force, (("gz", 2),), 3)
        smooth = planes_filter(force, GAUSS_TAPS, planes)
        smooth = along_cols(along_rows(smooth, gauss_rows), gauss_cols)
        local = smooth.reshape(3, slots, planes, coarse_rows, SCALE, coarse_cols, SCALE).sum(
            axis=(4, 6)
        )
        piece = jnp.einsum("kp,cspab->sckab", restrict, local, precision=EXACT).reshape(slots, -1)
        onehot_local = (positions[:, None] == block_place[None, :]).astype(jnp.float32)
        local_grid = jnp.dot(onehot_local, piece, precision=EXACT)
        total = lax.psum(local_grid, ("blk", "gz"))
        velocity = regularize(velocity, total, coarse_rows, coarse_cols)
        correlation = similar
    return (velocity, correlation)


def solution(mesh):
    return jax.shard_map(
        per_device,
        mesh=mesh,
        in_specs=(P("blk", "gz", None, None), P("blk", "gz", None, None), P("blk"), P("blk")),
        out_specs=(P(), P("blk", "gz", None, None)),
        check_vma=False,
    )
```

profile of v0, /device:TPU:1, one launch (start us, length us, event | category | flops | bytes accessed | tf_op | source)
XLA Modules:
  0.0 267.4 jit_solution(6952006898740505339)
XLA Ops:
  0.6 0.9 copy_bitcast_fusion
  1.6 4.0 %collective-permute-start = (bf16[2,1,5,32,128]{4,2,3,1,0:T(8,128)(2,1)S(1)}, bf16[2,1,5,32,128]{4,2,3,1,0:T(8,128)(2,1)S(1)}, u32[]{:S(2)}, u32[]{:S(2)}) collective-permute-start(bf16[2,1,5,32,128]{4,2,3,1,0:T(8,128)(2,1)S(1)} %get-tuple-element.38), channel_id=1, source_target_pairs={{0,1},{1,2},{2,3},{4,5},{5,6},{6,7},{8,9},{9,10},{10,11},{12,13},{... | collective-permute-start | bytes 245768 | tf_op jit(solution)/shard_map/ppermute | solution.py:23
  5.7 1.3 collective-permute-start.1
  9.3 0.9 fusion.94
  10.2 1.2 collective-permute-done.1
  13.3 1.0 fusion.6
  14.7 3.5 %collective-permute-start.2 = (f32[3,1,3,32,128]{4,2,3,1,0:T(4,128)S(1)}, f32[3,1,3,32,128]{4,2,3,1,0:T(4,128)S(1)}, u32[]{:S(2)}, u32[]{:S(2)}) collective-permute-start(f32[3,1,3,32,128]{4,2,3,1,0:T(4,128)S(1)} %get-tuple-element.30), channel_id=1, source_target_pairs={{0,1},{1,2},{2,3},{4,5},{5,6},{6,7},{8,9},{9,10},{10,11},{12,13},{... | collective-permute-start | bytes 442376 | tf_op jit(solution)/shard_map/ppermute | solution.py:23
  18.2 1.3 collective-permute-start.3
  19.6 1.3 collective-permute-done.2
  20.8 3.8 %collective-permute-done.3 = f32[3,1,3,32,128]{4,2,3,1,0:T(4,128)S(1)} collective-permute-done((f32[3,1,3,32,128]{4,2,3,1,0:T(4,128)S(1)}, f32[3,1,3,32,128]{4,2,3,1,0:T(4,128)S(1)}, u32[]{:S(2)}, u32[]{:S(2)}) %collective-permute-start.3) | collective-permute-done | bytes 147488 | tf_op jit(solution)/shard_map/ppermute | solution.py:26
  25.6 3.3 %convolution_reduce_fusion.1 = f32[3,8,2,8]{3,2,1,0:T(2,128)S(1)} fusion(f32[3,8,2,16,128,1]{4,3,5,2,1,0:T(8,128)S(1)} %bitcast.237, f32[8,16,128,1,1,1]{2,1,0,5,4,3:T(8,128)S(1)} %bitcast.238), kind=kOutput, calls=%fused_computation.1 | convolution fusion | flops 151092864 | bytes 460288 | tf_op jit(solution)/shard_map/...y,yv->...v/dot_general | solution.py:46
  29.7 1.2 copy.70
  31.0 1.4 reshape.690
  32.3 111.2 %psum.14 = f32[3,2,32,64]{3,2,1,0:T(8,128)S(1)} all-reduce(f32[3,2,32,64]{3,2,1,0:T(8,128)S(1)} %reshape.690), channel_id=1, replica_groups=mesh['blk'=128,'gz'=4] {'blk','gz'}, use_global_device_ids=true, to_apply=%region_1.2 | all-reduce | flops 12288 | bytes 98304 | tf_op jit(solution)/shard_map/psum | solution.py:180
  143.6 0.7 multiply_reduce_fusion.1
  145.8 0.9 convolution_bitcast_fusion
  148.2 1.0 fusion.4
  149.7 1.4 collective-permute-start.4
  151.1 1.3 collective-permute-start.5
  153.1 1.5 collective-permute-done.4
  154.6 3.8 %collective-permute-done.5 = f32[3,1,3,32,128]{4,2,3,1,0:T(4,128)S(1)} collective-permute-done((f32[3,1,3,32,128]{4,2,3,1,0:T(4,128)S(1)}, f32[3,1,3,32,128]{4,2,3,1,0:T(4,128)S(1)}, u32[]{:S(2)}, u32[]{:S(2)}) %collective-permute-start.5) | collective-permute-done | bytes 147488 | tf_op jit(solution)/shard_map/ppermute | solution.py:26
  159.3 3.3 %convolution_reduce_fusion = f32[3,8,2,8]{3,2,1,0:T(2,128)S(1)} fusion(f32[3,8,2,16,128,1]{4,3,5,2,1,0:T(8,128)S(1)} %bitcast.236, f32[8,16,128,1,1,1]{2,1,0,5,4,3:T(8,128)S(1)} %bitcast.239), kind=kOutput, calls=%fused_computation | convolution fusion | flops 151092864 | bytes 460288 | tf_op jit(solution)/shard_map/...y,yv->...v/dot_general | solution.py:46
  164.0 101.1 %psum.15 = f32[3,2,32,64]{3,2,1,0:T(8,128)S(1)} all-reduce(f32[3,2,32,64]{3,2,1,0:T(8,128)S(1)} %reshape.698), channel_id=1, replica_groups=mesh['blk'=128,'gz'=4] {'blk','gz'}, use_global_device_ids=true, to_apply=%region_4.5 | all-reduce | flops 12288 | bytes 98304 | tf_op jit(solution)/shard_map/psum | solution.py:180
  266.6 0.8 divide_add_fusion
  (75 shorter events, 11.2 us)
Async XLA Ops:
  1.6 8.6 %collective-permute-start = (bf16[2,1,5,32,128]{4,2,3,1,0:T(8,128)(2,1)S(1)}, bf16[2,1,5,32,128]{4,2,3,1,0:T(8,128)(2,1)S(1)}, u32[]{:S(2)}, u32[]{:S(2)}) collective-permute-start(bf16[2,1,5,32,128]{4,2,3,1,0:T(8,128)(2,1)S(1)} %get-tuple-element.38), channel_id=1, source_target_pairs={{0,1},{1,2},{2,3},{4,5},{5,6},{6,7},{8,9},{9,10},{10,11},{12,13},{... | collective-permute-start | bytes 245768 | tf_op jit(solution)/shard_map/ppermute | solution.py:23
  5.7 5.7 %collective-permute-start.1 = (bf16[2,1,5,32,128]{4,2,3,1,0:T(8,128)(2,1)S(1)}, bf16[2,1,5,32,128]{4,2,3,1,0:T(8,128)(2,1)S(1)}, u32[]{:S(2)}, u32[]{:S(2)}) collective-permute-start(bf16[2,1,5,32,128]{4,2,3,1,0:T(8,128)(2,1)S(1)} %get-tuple-element.39), channel_id=1, source_target_pairs={{1,0},{2,1},{3,2},{5,4},{6,5},{7,6},{9,8},{10,9},{11,10},{13,12},{... | collective-permute-start | bytes 245768 | tf_op jit(solution)/shard_map/ppermute | solution.py:26
  7.6 2.6 copy-start
  7.8 2.4 copy-start.2
  14.7 6.1 %collective-permute-start.2 = (f32[3,1,3,32,128]{4,2,3,1,0:T(4,128)S(1)}, f32[3,1,3,32,128]{4,2,3,1,0:T(4,128)S(1)}, u32[]{:S(2)}, u32[]{:S(2)}) collective-permute-start(f32[3,1,3,32,128]{4,2,3,1,0:T(4,128)S(1)} %get-tuple-element.30), channel_id=1, source_target_pairs={{0,1},{1,2},{2,3},{4,5},{5,6},{6,7},{8,9},{9,10},{10,11},{12,13},{... | collective-permute-start | bytes 442376 | tf_op jit(solution)/shard_map/ppermute | solution.py:23
  18.2 6.4 %collective-permute-start.3 = (f32[3,1,3,32,128]{4,2,3,1,0:T(4,128)S(1)}, f32[3,1,3,32,128]{4,2,3,1,0:T(4,128)S(1)}, u32[]{:S(2)}, u32[]{:S(2)}) collective-permute-start(f32[3,1,3,32,128]{4,2,3,1,0:T(4,128)S(1)} %get-tuple-element.31), channel_id=1, source_target_pairs={{1,0},{2,1},{3,2},{5,4},{6,5},{7,6},{9,8},{10,9},{11,10},{13,12},{... | collective-permute-start | bytes 442376 | tf_op jit(solution)/shard_map/ppermute | solution.py:26
  29.7 115.3 %copy-start.1 = (f32[32]{0:T(128)S(1)}, f32[32]{0:T(128)}, u32[]{:S(2)}) copy-start(f32[32]{0:T(128)} %copy-done) | copy-start | bytes 388
  29.7 115.3 %copy-start.3 = (f32[32]{0:T(128)S(1)}, f32[32]{0:T(128)}, u32[]{:S(2)}) copy-start(f32[32]{0:T(128)} %copy-done.2) | copy-start | bytes 388
  149.7 4.9 %collective-permute-start.4 = (f32[3,1,3,32,128]{4,2,3,1,0:T(4,128)S(1)}, f32[3,1,3,32,128]{4,2,3,1,0:T(4,128)S(1)}, u32[]{:S(2)}, u32[]{:S(2)}) collective-permute-start(f32[3,1,3,32,128]{4,2,3,1,0:T(4,128)S(1)} %get-tuple-element.26), channel_id=1, source_target_pairs={{0,1},{1,2},{2,3},{4,5},{5,6},{6,7},{8,9},{9,10},{10,11},{12,13},{... | collective-permute-start | bytes 442376 | tf_op jit(solution)/shard_map/ppermute | solution.py:23
  151.1 7.3 %collective-permute-start.5 = (f32[3,1,3,32,128]{4,2,3,1,0:T(4,128)S(1)}, f32[3,1,3,32,128]{4,2,3,1,0:T(4,128)S(1)}, u32[]{:S(2)}, u32[]{:S(2)}) collective-permute-start(f32[3,1,3,32,128]{4,2,3,1,0:T(4,128)S(1)} %get-tuple-element.27), channel_id=1, source_target_pairs={{1,0},{2,1},{3,2},{5,4},{6,5},{7,6},{9,8},{10,9},{11,10},{13,12},{... | collective-permute-start | bytes 442376 | tf_op jit(solution)/shard_map/ppermute | solution.py:26
where the time goes:
time: 268 us; the launch traced here: 267 us
  blocking collectives  212 us (79%)
  matrix products  14.4 us (5%)
  starting transfers between devices  12.8 us (5%)
  waiting for transfers between devices  11.6 us (4%)
  local copies, waits for them, and re-layouts  6.26 us (2%)
  other arithmetic  6.11 us (2%)
  between operations  3.95 us (1%)
    psum x2, blocking collectives, per_device(): total = lax.psum(local_grid, ('blk', 'gz'))  212 us
    ppermute x3, starting transfers between devices, with_halo(): lax.ppermute(lax.slice_in_dim(block, block.shape[dim] - width, None, axis...  8.92 us
    ppermute x3, waiting for transfers between devices, with_halo(): lax.ppermute(lax.slice_in_dim(block, 0, width, axis=dim), axis, backward)  8.79 us
    dot_general x4, matrix products, along_cols(): return jnp.einsum('...y,yv->...v', field, matrix, precision=EXACT)  8.73 us
  transfers between devices with their start and end apart: 6, of which 5 were waited for; matrix products, arithmetic and copies ran while one was open for 1% of the time, Pallas kernels for 0%

commit v1 on v0

--- a/solution.py
+++ b/solution.py
@@ -177,7 +177,7 @@
         piece = jnp.einsum("kp,cspab->sckab", restrict, local, precision=EXACT).reshape(slots, -1)
         onehot_local = (positions[:, None] == block_place[None, :]).astype(jnp.float32)
         local_grid = jnp.dot(onehot_local, piece, precision=EXACT)
-        total = lax.psum(local_grid, ("blk", "gz"))
+        total = jnp.sum(lax.all_gather(local_grid, ("blk", "gz")), axis=0)
         velocity = regularize(velocity, total, coarse_rows, coarse_cols)
         correlation = similar
     return (velocity, correlation)

time: 268 us -> 603 us (2.25)
  waiting for transfers between devices: 11.6 us -> 509 us
  blocking collectives: 212 us -> 0 us
  local copies, waits for them, and re-layouts: 6.26 us -> 32.9 us
  between operations: 3.95 us -> 17.4 us
  other arithmetic: 6.11 us -> 13.4 us
    all_gather x0 -> x2, waiting for transfers between devices: none -> 496 us  [per_device(): total = jnp.sum(lax.all_gather(local_grid, ('blk', 'gz')), axis=0)]
    psum x2 -> x0, blocking collectives: 212 us -> none  [per_device(): total = lax.psum(local_grid, ('blk', 'gz'))]
    unnamed x10 -> x12, local copies, waits for them, and re-layouts: 0.82 us -> 27.5 us
  transfers between devices with their start and end apart: 6 -> 8, of which waited for: 5 -> 7; matrix products, arithmetic and copies ran while one was open for 1% -> 0% of each run, Pallas kernels for 0% -> 0%
where the time goes in v1:
time: 603 us; the launch traced here: 602 us
  waiting for transfers between devices  509 us (84%)
  local copies, waits for them, and re-layouts  32.9 us (5%)
  between operations  17.4 us (3%)
  starting transfers between devices  15 us (2%)
  matrix products  14.4 us (2%)
  other arithmetic  13.4 us (2%)
    all_gather x2, waiting for transfers between devices, per_device(): total = jnp.sum(lax.all_gather(local_grid, ('blk', 'gz')), axis=0)  496 us
    unnamed x12, local copies, waits for them, and re-layouts  27.5 us
  transfers between devices with their start and end apart: 8, of which 7 were waited for; matrix products, arithmetic and copies ran while one was open for 0% of the time, Pallas kernels for 0%

profile of v1, /device:TPU:1, one launch (start us, length us, event | category | flops | bytes accessed | tf_op | source)
XLA Modules:
  0.0 601.6 jit_solution(15449223172951348866)
XLA Ops:
  7.2 0.9 copy_bitcast_fusion
  8.2 4.0 collective-permute-start
  12.2 1.3 collective-permute-start.1
  16.8 1.2 collective-permute-done.1
  19.9 1.0 fusion.6
  21.3 3.5 collective-permute-start.2
  24.8 1.3 collective-permute-start.3
  26.2 1.3 collective-permute-done.2
  27.4 3.8 collective-permute-done.3
  32.2 3.3 convolution_reduce_fusion.1
  36.8 251.7 %all-gather.5.cloned.1.call-done = f32[65536,96]{0,1:T(8,128)} async-done(((f32[128,96]{0,1:T(8,128)}), f32[65536,96]{0,1:T(8,128)}) %all-gather.5.cloned.1.call-update) | async-done | bytes 25165840 | tf_op jit(solution)/shard_map/all_gather | solution.py:180
  288.5 13.3 %copy.108 = f32[12,8,512,128]{3,2,1,0:T(8,128)S(1)} copy(f32[12,8,512,128]{3,1,2,0:T(8,128)} %bitcast.243) | data formatting | bytes 50331648
  301.8 3.0 bitcast_reduce_fusion.1
  305.3 1.3 copy.71
  306.5 1.4 reshape.690
  312.6 1.0 fusion.4
  314.0 3.1 collective-permute-start.4
  317.2 1.5 collective-permute-start.5
  318.7 2.5 collective-permute-done.4
  321.2 3.8 collective-permute-done.5
  325.9 3.3 convolution_reduce_fusion
  330.9 244.2 %all-gather.7.cloned.1.call-done = f32[65536,96]{0,1:T(8,128)} async-done(((f32[128,96]{0,1:T(8,128)}), f32[65536,96]{0,1:T(8,128)}) %all-gather.7.cloned.1.call-update) | async-done | bytes 25165840 | tf_op jit(solution)/shard_map/all_gather | solution.py:180
  575.1 13.3 %copy.109 = f32[12,8,512,128]{3,2,1,0:T(8,128)S(1)} copy(f32[12,8,512,128]{3,1,2,0:T(8,128)} %bitcast.242) | data formatting | bytes 50331648
  588.5 3.0 bitcast_reduce_fusion
  (83 shorter events, 16.1 us)
Async XLA Ops:
  7.2 281.3 %all-gather.5.cloned.1.call-start = ((), (), s32[]{:S(2)}) async-start(), calls=%async_computation | async-start | bytes 25214976 | tf_op jit(solution)/shard_map/all_gather | solution.py:180
  8.2 8.6 %collective-permute-start = (bf16[2,1,5,32,128]{4,2,3,1,0:T(8,128)(2,1)S(1)}, bf16[2,1,5,32,128]{4,2,3,1,0:T(8,128)(2,1)S(1)}, u32[]{:S(2)}, u32[]{:S(2)}) collective-permute-start(bf16[2,1,5,32,128]{4,2,3,1,0:T(8,128)(2,1)S(1)} %get-tuple-element.38), channel_id=1, source_target_pairs={{0,1},{1,2},{2,3},{4,5},{5,6},{6,7},{8,9},{9,10},{10,11},{12,13},{... | collective-permute-start | bytes 245768 | tf_op jit(solution)/shard_map/ppermute | solution.py:23
  12.2 5.7 collective-permute-start.1
  14.2 3.9 copy-start
  15.0 3.2 copy-start.2
  21.3 6.1 %collective-permute-start.2 = (f32[3,1,3,32,128]{4,2,3,1,0:T(4,128)S(1)}, f32[3,1,3,32,128]{4,2,3,1,0:T(4,128)S(1)}, u32[]{:S(2)}, u32[]{:S(2)}) collective-permute-start(f32[3,1,3,32,128]{4,2,3,1,0:T(4,128)S(1)} %get-tuple-element.30), channel_id=1, source_target_pairs={{0,1},{1,2},{2,3},{4,5},{5,6},{6,7},{8,9},{9,10},{10,11},{12,13},{... | collective-permute-start | bytes 442376 | tf_op jit(solution)/shard_map/ppermute | solution.py:23
  24.8 6.4 %collective-permute-start.3 = (f32[3,1,3,32,128]{4,2,3,1,0:T(4,128)S(1)}, f32[3,1,3,32,128]{4,2,3,1,0:T(4,128)S(1)}, u32[]{:S(2)}, u32[]{:S(2)}) collective-permute-start(f32[3,1,3,32,128]{4,2,3,1,0:T(4,128)S(1)} %get-tuple-element.31), channel_id=1, source_target_pairs={{1,0},{2,1},{3,2},{5,4},{6,5},{7,6},{9,8},{10,9},{11,10},{13,12},{... | collective-permute-start | bytes 442376 | tf_op jit(solution)/shard_map/ppermute | solution.py:26
  36.5 538.6 %all-gather.7.cloned.1.call-start = ((), (), s32[]{:S(2)}) async-start(), calls=%async_computation.1 | async-start | bytes 25214976 | tf_op jit(solution)/shard_map/all_gather | solution.py:180
  305.3 4.1 copy-start.1
  305.3 4.1 copy-start.3
  314.0 7.1 %collective-permute-start.4 = (f32[3,1,3,32,128]{4,2,3,1,0:T(4,128)S(1)}, f32[3,1,3,32,128]{4,2,3,1,0:T(4,128)S(1)}, u32[]{:S(2)}, u32[]{:S(2)}) collective-permute-start(f32[3,1,3,32,128]{4,2,3,1,0:T(4,128)S(1)} %get-tuple-element.26), channel_id=1, source_target_pairs={{0,1},{1,2},{2,3},{4,5},{5,6},{6,7},{8,9},{9,10},{10,11},{12,13},{... | collective-permute-start | bytes 442376 | tf_op jit(solution)/shard_map/ppermute | solution.py:23
  317.2 7.8 %collective-permute-start.5 = (f32[3,1,3,32,128]{4,2,3,1,0:T(4,128)S(1)}, f32[3,1,3,32,128]{4,2,3,1,0:T(4,128)S(1)}, u32[]{:S(2)}, u32[]{:S(2)}) collective-permute-start(f32[3,1,3,32,128]{4,2,3,1,0:T(4,128)S(1)} %get-tuple-element.27), channel_id=1, source_target_pairs={{1,0},{2,1},{3,2},{5,4},{6,5},{7,6},{9,8},{10,9},{11,10},{13,12},{... | collective-permute-start | bytes 442376 | tf_op jit(solution)/shard_map/ppermute | solution.py:26
Sparse Core Ops, SparseCore 0:
  36.6 251.7 all-gather.4
  330.4 244.7 all-gather.6
